TPU v7x, 256 devices: a whole 4x4x8 slice. The times are simulated.
256 devices in a mesh: space: 8 (over z_hi, y), dp: 32 (over x, z_lo, core).
Axes of the slice: x: 4, y: 4, z: 8 (z_hi: 2, z_lo: 4; z = z_hi * 4 + z_lo), core: 2. Of those that a mesh axis runs over, the one named last changes fastest.
Arguments:
- features: bfloat16 [32, 48, 64, 8, 128], P('dp', None, 'space'), may hold values from -21 to 21
- upstream: bfloat16 [32, 48, 64, 8, 128], P('dp', None, 'space'), may hold values from -21 to 21
- weight_one: bfloat16 [48, 48, 3, 3, 3], replicated, may hold values from -0.15625 to 0.15625
- weight_two: bfloat16 [48, 48, 3, 3, 3], replicated, may hold values from -0.15625 to 0.15625
- norm_gain: float32 [48], replicated, may hold values from 0.25 to 1.75
- norm_bias: float32 [48], replicated, may hold values from -3 to 3
Outputs:
- grad_input: bfloat16 [32, 48, 64, 8, 128], P('dp', None, 'space')
- grad_one: float32 [48, 48, 3, 3, 3], replicated
- grad_two: float32 [48, 48, 3, 3, 3], replicated
- grad_gain: float32 [48], replicated
- grad_bias: float32 [48], replicated
All inputs are finite; a program needn't handle non-finite values.
Results may differ from a plain program's by a relative error of at most 0.0029.
Values may be sent and summed in bfloat16 or wider, within the bound.
A program may use at most 128 MiB of HBM per device.

v0:
```python
import jax
import jax.numpy as jnp
from jax import lax
from jax.sharding import PartitionSpec as P

epsilon = 1e-05


def padded_2(cells, sides, width):
    for axis, dim in sides:
        count = lax.axis_size(axis)
        ends = count - 1
        head = lax.slice_in_dim(cells, 0, width, axis=dim)
        tail = lax.slice_in_dim(cells, cells.shape[dim] - width, cells.shape[dim], axis=dim)
        cells = jnp.concatenate(
            [
                lax.ppermute(tail, axis, [(i, (i + 1) % count) for i in range(ends)]),
                cells,
                lax.ppermute(head, axis, [((i + 1) % count, i) for i in range(ends)]),
            ],
            axis=dim,
        )
    return cells


def slab_faces(field):
    return padded_2(field, (("space", 2),), 1)


def conv_slab(padded, kernel):
    return lax.conv_general_dilated(
        padded,
        kernel,
        (1, 1, 1),
        ((0, 0), (1, 1), (1, 1)),
        dimension_numbers=("NCDHW", "OIDHW", "NCDHW"),
        preferred_element_type=jnp.float32,
    )


def flipped(kernel):
    return jnp.transpose(kernel, (1, 0, 2, 3, 4))[:, :, ::-1, ::-1, ::-1]


def kernel_grad(padded, target):
    return lax.conv_general_dilated(
        padded,
        target,
        (1, 1, 1),
        ((0, 0), (1, 1), (1, 1)),
        dimension_numbers=("CNDHW", "IODHW", "CNDHW"),
        preferred_element_type=jnp.float32,
    )


def local(features, upstream, weight_one, weight_two, norm_gain, norm_bias):
    axes_cells = (2, 3, 4)
    cells_all = float(
        features.shape[2] * features.shape[3] * features.shape[4] * lax.axis_size("space")
    )
    padded_x = slab_faces(features)
    pre_act = conv_slab(padded_x, weight_one)
    sums_pre, squares_pre = lax.psum(
        (
            jnp.sum(pre_act, axis=axes_cells, keepdims=True),
            jnp.sum(pre_act * pre_act, axis=axes_cells, keepdims=True),
        ),
        "space",
    )
    mean_pre = sums_pre / cells_all
    inv_std = lax.rsqrt(squares_pre / cells_all - mean_pre * mean_pre + epsilon)
    normal_hat = (pre_act - mean_pre) * inv_std
    gain_b = norm_gain.reshape(1, -1, 1, 1, 1)
    normed = normal_hat * gain_b + norm_bias.reshape(1, -1, 1, 1, 1)
    sigmoid_val = jax.nn.sigmoid(normed)
    hidden = (normed * sigmoid_val).astype(jnp.bfloat16)
    padded_h = slab_faces(hidden)
    padded_g = slab_faces(upstream)
    local_two = kernel_grad(padded_h, upstream)
    grad_hidden = conv_slab(padded_g, flipped(weight_two))
    grad_norm = grad_hidden * sigmoid_val * (1.0 + normed * (1.0 - sigmoid_val))
    local_bias = jnp.sum(grad_norm, axis=(0, 2, 3, 4))
    local_gain = jnp.sum(grad_norm * normal_hat, axis=(0, 2, 3, 4))
    slope_sum, slope_dot = lax.psum(
        (
            jnp.sum(grad_norm, axis=axes_cells, keepdims=True),
            jnp.sum(grad_norm * normal_hat, axis=axes_cells, keepdims=True),
        ),
        "space",
    )
    grad_pre = (
        gain_b
        * inv_std
        * (grad_norm - slope_sum / cells_all - normal_hat * (slope_dot / cells_all))
    ).astype(jnp.bfloat16)
    padded_grad = slab_faces(grad_pre)
    local_one = kernel_grad(padded_x, grad_pre)
    back = conv_slab(padded_grad, flipped(weight_one))
    grad_input = (upstream.astype(jnp.float32) + back).astype(jnp.bfloat16)
    grad_one, grad_two, grad_gain, grad_bias = lax.psum(
        (local_one, local_two, local_gain, local_bias), ("space", "dp")
    )
    return (grad_input, grad_one, grad_two, grad_gain, grad_bias)


def solution(mesh):
    in_specs = (
        P("dp", None, "space", None, None),
        P("dp", None, "space", None, None),
        P(),
        P(),
        P(),
        P(),
    )
    out_specs = (P("dp", None, "space", None, None), P(), P(), P(), P())
    return jax.shard_map(local, mesh=mesh, in_specs=in_specs, out_specs=out_specs, check_vma=False)
```

profile of v0, /device:TPU:1, one launch (start us, length us, event | category | flops | bytes accessed | tf_op | source)
XLA Modules:
  0.0 684.3 jit_solution(1534281291638809892)
XLA Ops:
  7.2 1.0 fusion.73
  8.3 4.2 collective-permute-start
  12.5 1.3 collective-permute-start.1
  13.8 1.6 fusion.74
  15.4 4.6 collective-permute-start.2
  20.0 1.3 collective-permute-start.3
  21.3 7.4 %copy.112 = bf16[1,48,8,8,128]{1,0,4,3,2:T(2,128)(2,1)} copy(bf16[1,48,8,8,128]{4,3,2,1,0:T(8,128)(2,1)} %param.7) | data formatting | bytes 1572864 | tf_op args[1]
  28.7 2.5 copy.85
  31.3 3.5 copy.86
  34.8 3.6 fusion.70
  38.4 3.1 fusion.68
  42.1 1.5 copy-done.10
  43.6 0.8 slice.50
  44.4 2.0 pad_maximum_fusion.3
  46.5 4.9 copy.89
  51.3 2.3 pad.2
  53.7 0.5 copy.91
  54.2 0.8 slice.51
  55.0 1.2 copy-done.11
  56.6 12.1 %select_reduce_fusion.3 = (f32[48]{0:T(128)S(1)}, f32[48]{0:T(128)S(1)}, f32[8,8,8,17,48]{4,2,3,1,0:T(8,128)}) fusion(pred[8,17]{0,1:T(8,128)(4,1)S(1)} %copy-done.14, bf16[48,48,3,3,3]{1,0,4,3,2:T(8,128)(2,1)S(1)} %copy-done, bf16[48,10,8,1,7,2]{0,4,5,2,1,3:T(8,128)(2,1)S(1)} %copy-done.13, bf16[48,10,8,1,8,17]{0,4,5,2,1,3:T(8,128)(2,1)S(1)} %copy-done.11), kind=kOutput, calls=%fused_computation.25 | convolution fusion | flops 998682496 | bytes 2948104 | tf_op jit(solution)/shard_map/conv_general_dilated | solution.py:31
  68.7 30.8 %all-reduce.3 = (f32[1,48,1,1,1]{1,4,3,2,0:T(1,128)S(1)}, f32[1,48,1,1,1]{1,4,3,2,0:T(1,128)S(1)}) all-reduce(f32[1,48,1,1,1]{1,4,3,2,0:T(1,128)S(1)} %bitcast.113, f32[1,48,1,1,1]{1,4,3,2,0:T(1,128)S(1)} %bitcast.112), channel_id=1, replica_groups=mesh['space'=8,'dp'=32] {'space'}, use_global_device_ids=true, to_apply=%region_1.0 | all-reduce | flops 96 | bytes 768 | tf_op jit(solution)/shard_map/psum | solution.py:63
  99.5 16.4 %select_reduce_fusion = (f32[48]{0:T(128)S(1)}, f32[48]{0:T(128)S(1)}, f32[8,8,8,17,48]{4,2,3,1,0:T(8,128)}) fusion(pred[8,17]{0,1:T(8,128)(4,1)S(1)} %copy-done.14, f32[48]{0:T(128)S(1)} %bitcast.108, f32[48]{0:T(128)S(1)} %get-tuple-element.55, f32[8,8,8,17,48]{4,2,3,1,0:T(8,128)} %get-tuple-element.56, f32[48]{0:T(128)S(1)} %copy-done.16, ...), kind=kOutput, calls=%fused_computation.17 | convolution fusion | flops 1004113792 | bytes 4620040 | tf_op jit(solution)/shard_map/conv_general_dilated | solution.py:31
  115.9 25.0 %all-reduce.2 = (f32[1,48,1,1,1]{1,4,3,2,0:T(1,128)S(1)}, f32[1,48,1,1,1]{1,4,3,2,0:T(1,128)S(1)}) all-reduce(f32[1,48,1,1,1]{1,4,3,2,0:T(1,128)S(1)} %bitcast.111, f32[1,48,1,1,1]{1,4,3,2,0:T(1,128)S(1)} %bitcast.110), channel_id=1, replica_groups=mesh['space'=8,'dp'=32] {'space'}, use_global_device_ids=true, to_apply=%region_5.0 | all-reduce | flops 96 | bytes 768 | tf_op jit(solution)/shard_map/psum | solution.py:84
  140.9 4.9 multiply_convert_fusion.1
  146.3 1.2 copy.128
  147.5 2.2 collective-permute-start.6
  149.8 1.2 copy.127
  151.0 1.3 collective-permute-start.7
  152.3 2.3 copy.117
  154.6 2.3 copy.118
  156.9 1.9 copy.104
  159.0 4.0 collective-permute-start.4
  163.0 1.3 collective-permute-start.5
  164.3 1.5 fusion.36
  165.9 17.9 %fusion.49 = f32[48,48,3,3,3]{0,1,4,3,2:T(8,128)} fusion(bf16[8,8,8,17,48]{4,2,3,1,0:T(8,128)(2,1)S(1)} %get-tuple-element.40, pred[8,17]{0,1:T(8,128)(4,1)S(1)} %copy-done.14, bf16[48,10,8,8,17,1]{0,3,5,4,2,1:T(8,128)(2,1)S(1)} %get-tuple-element.60, bf16[48,10,8,8,17,1]{0,3,5,4,2,1:T(8,128)(2,1)} %copy.104, ...), kind=kOutput, calls=%fused_computation.61 | convolution fusion | flops 1002491904 | bytes 4217992 | tf_op jit(solution)/shard_map/conv_general_dilated | solution.py:46
  184.3 6.4 copy.126
  190.7 101.2 %all-reduce = (f32[48]{0:T(128)}, f32[48]{0:T(128)}) all-reduce(f32[48]{0:T(128)S(1)} %get-tuple-element.25, f32[48]{0:T(128)S(1)} %get-tuple-element.26), channel_id=1, replica_groups=mesh['space'=8,'dp'=32] {'space','dp'}, use_global_device_ids=true, to_apply=%region_10.0 | all-reduce | flops 96 | bytes 768 | tf_op jit(solution)/shard_map/psum | solution.py:100
  291.9 0.6 maximum_bitcast_fusion
  292.5 0.6 pad.7
  293.7 10.5 %broadcast_select_fusion = f32[8,8,8,17,48]{4,2,3,1,0:T(8,128)S(1)} fusion(pred[8,17]{0,1:T(8,128)(4,1)S(1)} %copy-done.14, bf16[48,48,3,3,3]{1,0,4,3,2:T(8,128)(2,1)S(1)} %copy-done, bf16[48,10,8,1,7,2]{0,4,5,2,1,3:T(8,128)(2,1)S(1)} %slice.57, bf16[48,10,8,1,8,17]{0,4,5,2,1,3:T(8,128)(2,1)S(1)} %copy.98), kind=kOutput, calls=%fused_computation.55 | convolution fusion | flops 996593664 | bytes 2947720 | tf_op jit(solution)/shard_map/conv_general_dilated | solution.py:31
  304.2 3.1 copy.99
  307.4 1.8 copy-done.8
  309.3 110.6 %fusion.11 = f32[48,48,3,3,3]{0,1,4,3,2:T(8,128)} fusion(bf16[1,48,8,8,128]{1,0,4,3,2:T(2,128)(2,1)S(1)} %copy-done.7, bf16[1,48,1,8,128]{1,0,4,3,2:T(2,128)(2,1)} %collective-permute-done.7, bf16[1,48,8,8,128]{1,0,4,3,2:T(2,128)(2,1)S(1)} %bitcast.102, bf16[1,48,1,8,128]{1,0,4,3,2:T(2,128)(2,1)} %collective-permute-done.6), kind=kOutput, calls=%fused_computation.15 | convolution fusion | flops 932364288 | bytes 2018304 | tf_op jit(solution)/shard_map/conv_general_dilated | solution.py:46
  419.9 4.1 fusion.13
  424.0 3.8 copy.113
  427.8 245.1 %all-reduce.6.cloned.1.call-done = (f32[48,48,3,3,3]{0,1,4,3,2:T(8,128)}, f32[48,48,3,3,3]{0,1,4,3,2:T(8,128)}) async-done(((f32[48,48,3,3,3]{0,1,4,3,2:T(8,128)}, f32[48,48,3,3,3]{0,1,4,3,2:T(8,128)}), (f32[48,48,3,3,3]{0,1,4,3,2:T(8,128)}, f32[48,48,3,3,3]{0,1,4,3,2:T(8,128)})) %all-reduce.6.cloned.1.call-update) | async-done | bytes 497680 | tf_op jit(solution)/shard_map/psum | solution.py:100
  672.9 2.2 copy.114
  675.1 2.2 copy.115
  (64 shorter events, 3.1 us)
Async XLA Ops:
  7.2 47.9 %copy-start = (bf16[48,48,3,3,3]{1,0,4,3,2:T(8,128)(2,1)S(1)}, bf16[48,48,3,3,3]{1,0,4,3,2:T(8,128)(2,1)}, u32[]{:S(2)}) copy-start(bf16[48,48,3,3,3]{1,0,4,3,2:T(8,128)(2,1)} %param.8) | copy-start | bytes 373252
  7.2 21.5 %copy-start.5 = (bf16[1,48,8,8,128]{4,3,2,1,0:T(8,128)(2,1)S(1)}, bf16[1,48,8,8,128]{4,3,2,1,0:T(8,128)(2,1)}, u32[]{:S(2)}) copy-start(bf16[1,48,8,8,128]{4,3,2,1,0:T(8,128)(2,1)} %param.7) | copy-start | bytes 2359300
  7.2 665.7 %all-reduce.6.cloned.1.call-start = ((), (), s32[]{:S(2)}) async-start(), calls=%async_computation | async-start | bytes 2654208 | tf_op jit(solution)/shard_map/psum | solution.py:100
  8.3 22.9 %copy-start.12 = (bf16[1,48,8,8,128]{4,3,2,1,0:T(8,128)(2,1)S(1)}, bf16[1,48,8,8,128]{4,3,2,1,0:T(8,128)(2,1)}, u32[]{:S(2)}) copy-start(bf16[1,48,8,8,128]{4,3,2,1,0:T(8,128)(2,1)} %param.6) | copy-start | bytes 2359300
  8.3 22.9 %collective-permute-start = (bf16[1,48,1,8,128]{4,3,2,1,0:T(8,128)(2,1)S(1)}, bf16[1,48,1,8,128]{4,3,2,1,0:T(8,128)(2,1)S(1)}, u32[]{:S(2)}, u32[]{:S(2)}) collective-permute-start(bf16[1,48,1,8,128]{4,3,2,1,0:T(8,128)(2,1)S(1)} %get-tuple-element.51), channel_id=1, source_target_pairs={{0,32},{32,64},{64,96},{96,128},{128,160},{160,192},{192,224},{1,3... | collective-permute-start | bytes 294920 | tf_op jit(solution)/shard_map/ppermute | solution.py:17
  12.5 18.7 %collective-permute-start.1 = (bf16[1,48,1,8,128]{4,3,2,1,0:T(8,128)(2,1)S(1)}, bf16[1,48,1,8,128]{4,3,2,1,0:T(8,128)(2,1)S(1)}, u32[]{:S(2)}, u32[]{:S(2)}) collective-permute-start(bf16[1,48,1,8,128]{4,3,2,1,0:T(8,128)(2,1)S(1)} %get-tuple-element.52), channel_id=1, source_target_pairs={{32,0},{64,32},{96,64},{128,96},{160,128},{192,160},{224,192},{33,... | collective-permute-start | bytes 294920 | tf_op jit(solution)/shard_map/ppermute | solution.py:19
  15.4 29.1 %collective-permute-start.2 = (bf16[1,48,1,8,128]{4,3,2,1,0:T(8,128)(2,1)}, bf16[1,48,1,8,128]{4,3,2,1,0:T(8,128)(2,1)}, u32[]{:S(2)}, u32[]{:S(2)}) collective-permute-start(bf16[1,48,1,8,128]{4,3,2,1,0:T(8,128)(2,1)} %get-tuple-element.53), channel_id=1, source_target_pairs={{0,32},{32,64},{64,96},{96,128},{128,160},{160,192},{192,224},{1,3... | collective-permute-start | bytes 294920 | tf_op jit(solution)/shard_map/ppermute | solution.py:17
  20.0 24.4 %collective-permute-start.3 = (bf16[1,48,1,8,128]{4,3,2,1,0:T(8,128)(2,1)S(1)}, bf16[1,48,1,8,128]{4,3,2,1,0:T(8,128)(2,1)}, u32[]{:S(2)}, u32[]{:S(2)}) collective-permute-start(bf16[1,48,1,8,128]{4,3,2,1,0:T(8,128)(2,1)S(1)} %get-tuple-element.54), channel_id=1, source_target_pairs={{32,0},{64,32},{96,64},{128,96},{160,128},{192,160},{224,192},{33,... | collective-permute-start | bytes 294920 | tf_op jit(solution)/shard_map/ppermute | solution.py:19
  41.5 2.9 copy-start.6
  42.1 1.6 copy-start.10
  53.7 2.6 copy-start.11
  53.7 2.8 copy-start.13
  53.7 2.8 copy-start.14
  54.2 14.5 %copy-start.9 = (bf16[48,10,8,1,8,17]{0,4,5,2,1,3:T(8,128)(2,1)}, bf16[48,10,8,1,8,17]{0,4,5,2,1,3:T(8,128)(2,1)S(1)}, u32[]{:S(2)}) copy-start(bf16[48,10,8,1,8,17]{0,4,5,2,1,3:T(8,128)(2,1)S(1)} %copy.91) | copy-start | bytes 3133444
  56.5 43.0 %copy-start.15 = (f32[48]{0:T(128)S(1)}, f32[48]{0:T(128)}, u32[]{:S(2)}) copy-start(f32[48]{0:T(128)} %param.10) | copy-start | bytes 580
  56.5 43.0 %copy-start.16 = (f32[48]{0:T(128)S(1)}, f32[48]{0:T(128)}, u32[]{:S(2)}) copy-start(f32[48]{0:T(128)} %param.11) | copy-start | bytes 580
  145.8 6.5 copy-start.3
  146.2 8.3 %copy-start.2 = (bf16[48,10,8,1,8,16]{0,2,5,4,1,3:T(8,128)(2,1)S(1)}, bf16[48,10,8,1,8,16]{0,2,5,4,1,3:T(8,128)(2,1)}, u32[]{:S(2)}) copy-start(bf16[48,10,8,1,8,16]{0,2,5,4,1,3:T(8,128)(2,1)} %get-tuple-element.42) | copy-start | bytes 2949124
  147.5 159.8 %collective-permute-start.6 = (bf16[1,48,1,8,128]{1,0,4,3,2:T(2,128)(2,1)}, bf16[1,48,1,8,128]{1,0,4,3,2:T(2,128)(2,1)}, u32[]{:S(2)}, u32[]{:S(2)}) collective-permute-start(bf16[1,48,1,8,128]{1,0,4,3,2:T(2,128)(2,1)} %bitcast.90), channel_id=1, source_target_pairs={{0,32},{32,64},{64,96},{96,128},{128,160},{160,192},{192,224},{1,3... | collective-permute-start | bytes 294920 | tf_op jit(solution)/shard_map/ppermute | solution.py:17
  151.0 156.3 %collective-permute-start.7 = (bf16[1,48,1,8,128]{1,0,4,3,2:T(2,128)(2,1)}, bf16[1,48,1,8,128]{1,0,4,3,2:T(2,128)(2,1)}, u32[]{:S(2)}, u32[]{:S(2)}) collective-permute-start(bf16[1,48,1,8,128]{1,0,4,3,2:T(2,128)(2,1)} %bitcast.89), channel_id=1, source_target_pairs={{32,0},{64,32},{96,64},{128,96},{160,128},{192,160},{224,192},{33,... | collective-permute-start | bytes 294920 | tf_op jit(solution)/shard_map/ppermute | solution.py:19
  159.0 132.9 %collective-permute-start.4 = (bf16[1,48,1,8,128]{1,3,4,0,2:T(8,128)(2,1)S(1)}, bf16[1,48,1,8,128]{1,3,4,0,2:T(8,128)(2,1)S(1)}, u32[]{:S(2)}, u32[]{:S(2)}) collective-permute-start(bf16[1,48,1,8,128]{1,3,4,0,2:T(8,128)(2,1)S(1)} %slice_bitcast_fusion.3), channel_id=1, source_target_pairs={{0,32},{32,64},{64,96},{96,128},{128,160},{160,192},{192,224},{1,3... | collective-permute-start | bytes 294920 | tf_op jit(solution)/shard_map/ppermute | solution.py:17
  163.0 128.9 %collective-permute-start.5 = (bf16[1,48,1,8,128]{1,3,4,2,0:T(8,128)(2,1)S(1)}, bf16[1,48,1,8,128]{1,3,4,2,0:T(8,128)(2,1)S(1)}, u32[]{:S(2)}, u32[]{:S(2)}) collective-permute-start(bf16[1,48,1,8,128]{1,3,4,2,0:T(8,128)(2,1)S(1)} %slice_bitcast_fusion.2), channel_id=1, source_target_pairs={{32,0},{64,32},{96,64},{128,96},{160,128},{192,160},{224,192},{33,... | collective-permute-start | bytes 294920 | tf_op jit(solution)/shard_map/ppermute | solution.py:19
  304.2 3.3 copy-start.7
  304.2 5.1 copy-start.8
  309.2 110.6 %copy-start.4 = (bf16[1,48,8,8,128]{1,3,4,2,0:T(8,128)(2,1)S(1)}, bf16[1,48,8,8,128]{1,3,4,2,0:T(8,128)(2,1)}, u32[]{:S(2)}) copy-start(bf16[1,48,8,8,128]{1,3,4,2,0:T(8,128)(2,1)} %copy.85) | copy-start | bytes 2359300
  419.9 257.4 %copy-start.1 = (bf16[48,48,3,3,3]{1,0,4,3,2:T(8,128)(2,1)S(1)}, bf16[48,48,3,3,3]{1,0,4,3,2:T(8,128)(2,1)}, u32[]{:S(2)}) copy-start(bf16[48,48,3,3,3]{1,0,4,3,2:T(8,128)(2,1)} %param.8) | copy-start | bytes 373252
Sparse Core Ops, SparseCore 0:
  420.0 252.9 all-reduce.5
where the time goes:
time: 690 us; the launch traced here: 684 us
  waiting for transfers between devices  245 us (36%)
  matrix products  167 us (24%)
  blocking collectives  157 us (23%)
  local copies, waits for them, and re-layouts  66.6 us (10%)
  starting transfers between devices  20.2 us (3%)
  between operations  14.7 us (2%)
  other arithmetic  13.3 us (2%)
    psum x1, waiting for transfers between devices, local(): lax.psum((local_one, local_two, local_gain, local_bias), ('space', 'dp'))  245 us
    conv_general_dilated x2, matrix products, kernel_grad(): lax.conv_general_dilated(padded, target, (1, 1, 1), ((0, 0), (1, 1), (1,...  128 us
    psum x1, blocking collectives, local(): lax.psum((local_one, local_two, local_gain, local_bias), ('space', 'dp'))  101 us
    conv_general_dilated x3, matrix products, conv_slab(): lax.conv_general_dilated(padded, kernel, (1, 1, 1), ((0, 0), (1, 1), (1,...  39 us
    unnamed x46, local copies, waits for them, and re-layouts  36.6 us
    psum x1, blocking collectives, local(): lax.psum((jnp.sum(pre_act, axis=axes_cells, keepdims=True), jnp.sum(pre_a...  30.8 us
    psum x1, blocking collectives, local(): lax.psum((jnp.sum(grad_norm, axis=axes_cells, keepdims=True), jnp.sum(gra...  25 us
    concatenate x8, local copies, waits for them, and re-layouts, padded_2(): jnp.concatenate([lax.ppermute(tail, axis, [(i, (i + 1) % count) for i in...  20 us
  transfers between devices with their start and end apart: 9, of which 1 were waited for; matrix products, arithmetic and copies ran while one was open for 12% of the time, Pallas kernels for 0%

commit v1 on v0

--- a/solution.py
+++ b/solution.py
@@ -4,6 +4,11 @@
 from jax.sharding import PartitionSpec as P
 
 epsilon = 1e-05
+
+
+def one_after_other(array, axis_one, axis_two):
+    partial = lax.psum(array, axis_one)
+    return lax.psum(partial, axis_two)
 
 
 def padded_2(cells, sides, width):
@@ -97,8 +102,8 @@
     local_one = kernel_grad(padded_x, grad_pre)
     back = conv_slab(padded_grad, flipped(weight_one))
     grad_input = (upstream.astype(jnp.float32) + back).astype(jnp.bfloat16)
-    grad_one, grad_two, grad_gain, grad_bias = lax.psum(
-        (local_one, local_two, local_gain, local_bias), ("space", "dp")
+    grad_one, grad_two, grad_gain, grad_bias = one_after_other(
+        (local_one, local_two, local_gain, local_bias), "dp", "space"
     )
     return (grad_input, grad_one, grad_two, grad_gain, grad_bias)
 

time: 690 us -> 766 us (1.11)
  waiting for transfers between devices: 245 us -> 386 us
  matrix products: 167 us -> 130 us
  blocking collectives: 157 us -> 129 us
    psum x1 -> x2, waiting for transfers between devices: 245 us -> 386 us  [the longest x1 285 us: one_after_other(): partial = lax.psum(array, axis_one)]
    conv_general_dilated x2, matrix products: 128 us -> 91.3 us  [kernel_grad(): lax.conv_general_dilated(padded, target, (1, 1, 1), ((0, 0), (1, 1), (1,...]
    psum x1, blocking collectives: 101 us -> 72.3 us  [one_after_other(): partial = lax.psum(array, axis_one)]
    unnamed x46 -> x48, local copies, waits for them, and re-layouts: 36.6 us -> 34.2 us
  transfers between devices with their start and end apart: 9 -> 10, of which waited for: 1 -> 2; matrix products, arithmetic and copies ran while one was open for 12% -> 20% of each run, Pallas kernels for 0% -> 0%
where the time goes in v1:
time: 766 us; the launch traced here: 756 us
  waiting for transfers between devices  386 us (50%)
  matrix products  130 us (17%)
  blocking collectives  129 us (17%)
  local copies, waits for them, and re-layouts  65 us (8%)
  starting transfers between devices  21 us (3%)
  between operations  14.9 us (2%)
  other arithmetic  10.6 us (1%)
    psum x1, waiting for transfers between devices, one_after_other(): partial = lax.psum(array, axis_one)  285 us
    psum x1, waiting for transfers between devices, one_after_other(): return lax.psum(partial, axis_two)  101 us
    conv_general_dilated x2, matrix products, kernel_grad(): lax.conv_general_dilated(padded, target, (1, 1, 1), ((0, 0), (1, 1), (1,...  91.3 us
    psum x1, blocking collectives, one_after_other(): partial = lax.psum(array, axis_one)  72.3 us
    conv_general_dilated x3, matrix products, conv_slab(): lax.conv_general_dilated(padded, kernel, (1, 1, 1), ((0, 0), (1, 1), (1,...  38.6 us
    unnamed x48, local copies, waits for them, and re-layouts  34.2 us
    psum x1, blocking collectives, local(): lax.psum((jnp.sum(pre_act, axis=axes_cells, keepdims=True), jnp.sum(pre_a...  30.6 us
    psum x1, blocking collectives, local(): lax.psum((jnp.sum(grad_norm, axis=axes_cells, keepdims=True), jnp.sum(gra...  25.8 us
  transfers between devices with their start and end apart: 10, of which 2 were waited for; matrix products, arithmetic and copies ran while one was open for 20% of the time, Pallas kernels for 0%

profile of v1, /device:TPU:1, one launch (start us, length us, event | category | flops | bytes accessed | tf_op | source)
XLA Modules:
  0.0 756.5 jit_solution(9780317928570091704)
XLA Ops:
  7.2 1.0 fusion.73
  8.3 4.2 collective-permute-start
  12.5 1.3 collective-permute-start.1
  13.8 1.6 fusion.74
  15.4 4.6 collective-permute-start.2
  20.0 1.3 collective-permute-start.3
  21.3 7.4 copy.112
  28.7 2.5 copy.85
  31.4 3.5 copy.86
  34.8 3.6 fusion.70
  38.4 3.2 fusion.68
  42.1 1.5 copy-done.9
  43.6 0.8 slice.50
  44.5 2.0 pad_maximum_fusion.3
  46.5 5.1 copy.89
  51.6 2.3 pad.2
  54.5 0.8 slice.51
  55.3 1.2 copy-done.10
  56.8 12.2 %select_reduce_fusion.3 = (f32[48]{0:T(128)S(1)}, f32[48]{0:T(128)S(1)}, f32[8,8,8,17,48]{4,2,3,1,0:T(8,128)}) fusion(pred[8,17]{0,1:T(8,128)(4,1)S(1)} %copy-done.14, bf16[48,48,3,3,3]{1,0,4,3,2:T(8,128)(2,1)S(1)} %copy-done, bf16[48,10,8,1,7,2]{0,4,5,2,1,3:T(8,128)(2,1)S(1)} %copy-done.13, bf16[48,10,8,1,8,17]{0,4,5,2,1,3:T(8,128)(2,1)S(1)} %copy-done.10), kind=kOutput, calls=%fused_computation.25 | convolution fusion | flops 998682496 | bytes 2948104 | tf_op jit(solution)/shard_map/conv_general_dilated | solution.py:36
  69.0 30.6 %all-reduce.3 = (f32[1,48,1,1,1]{1,4,3,2,0:T(1,128)S(1)}, f32[1,48,1,1,1]{1,4,3,2,0:T(1,128)S(1)}) all-reduce(f32[1,48,1,1,1]{1,4,3,2,0:T(1,128)S(1)} %bitcast.112, f32[1,48,1,1,1]{1,4,3,2,0:T(1,128)S(1)} %bitcast.111), channel_id=1, replica_groups=mesh['space'=8,'dp'=32] {'space'}, use_global_device_ids=true, to_apply=%region_1.0 | all-reduce | flops 96 | bytes 768 | tf_op jit(solution)/shard_map/psum | solution.py:68
  99.6 16.4 %select_reduce_fusion = (f32[48]{0:T(128)S(1)}, f32[48]{0:T(128)S(1)}, f32[8,8,8,17,48]{4,2,3,1,0:T(8,128)}) fusion(pred[8,17]{0,1:T(8,128)(4,1)S(1)} %copy-done.14, f32[48]{0:T(128)S(1)} %bitcast.107, f32[48]{0:T(128)S(1)} %get-tuple-element.59, f32[8,8,8,17,48]{4,2,3,1,0:T(8,128)} %get-tuple-element.60, f32[48]{0:T(128)S(1)} %copy-done.17, ...), kind=kOutput, calls=%fused_computation.17 | convolution fusion | flops 1004113792 | bytes 4620040 | tf_op jit(solution)/shard_map/conv_general_dilated | solution.py:36
  116.0 72.3 %all-reduce = (f32[48]{0:T(128)S(1)}, f32[48]{0:T(128)S(1)}) all-reduce(f32[48]{0:T(128)S(1)} %get-tuple-element.25, f32[48]{0:T(128)S(1)} %get-tuple-element.26), channel_id=1, replica_groups=mesh['space'=8,'dp'=32] {'dp'}, use_global_device_ids=true, to_apply=%region_12.0 | all-reduce | flops 96 | bytes 768 | tf_op jit(solution)/shard_map/psum | solution.py:10
  188.2 25.8 %all-reduce.2 = (f32[1,48,1,1,1]{1,4,3,2,0:T(1,128)S(1)}, f32[1,48,1,1,1]{1,4,3,2,0:T(1,128)S(1)}, f32[48]{0:T(128)}, f32[48]{0:T(128)}) all-reduce(f32[1,48,1,1,1]{1,4,3,2,0:T(1,128)S(1)} %bitcast.110, f32[1,48,1,1,1]{1,4,3,2,0:T(1,128)S(1)} %bitcast.109, f32[48]{0:T(128)S(1)} %get-tuple-element.29, ...), channel_id=1, replica_groups=mesh['space'=8,'dp'=32] {'space'}, use_global_device_ids=true, to_apply=%region_5.0 | all-reduce | flops 192 | bytes 1536 | tf_op jit(solution)/shard_map/psum | solution.py:89
  214.0 4.9 multiply_convert_fusion.1
  218.9 1.7 copy.93
  220.8 1.2 copy.128
  222.0 2.1 collective-permute-start.6
  224.1 1.2 copy.127
  225.3 1.3 collective-permute-start.7
  226.6 2.3 copy.117
  228.9 2.3 copy.118
  231.3 1.9 copy.104
  233.3 0.7 slice_bitcast_fusion.3
  234.0 4.7 collective-permute-start.4
  239.5 1.5 collective-permute-start.5
  241.0 1.6 fusion.36
  242.6 16.3 %fusion.49 = f32[48,48,3,3,3]{0,1,4,3,2:T(8,128)} fusion(bf16[8,8,8,17,48]{4,2,3,1,0:T(8,128)(2,1)S(1)} %get-tuple-element.44, pred[8,17]{0,1:T(8,128)(4,1)S(1)} %copy-done.14, bf16[48,10,8,8,17,1]{0,3,5,4,2,1:T(8,128)(2,1)S(1)} %get-tuple-element.64, bf16[48,10,8,8,17,1]{0,3,5,4,2,1:T(8,128)(2,1)S(1)} %copy-done.11, ...), kind=kOutput, calls=%fused_computation.61 | convolution fusion | flops 1002491904 | bytes 4217992 | tf_op jit(solution)/shard_map/conv_general_dilated | solution.py:51
  259.3 6.3 copy.126
  265.7 75.0 %fusion.11 = f32[48,48,3,3,3]{0,1,4,3,2:T(8,128)} fusion(bf16[1,48,8,8,128]{1,0,4,3,2:T(2,128)(2,1)S(1)} %copy-done.7, bf16[1,48,1,8,128]{1,0,4,3,2:T(2,128)(2,1)} %collective-permute-done.7, bf16[1,48,8,8,128]{1,0,4,3,2:T(2,128)(2,1)} %bitcast.102, bf16[1,48,1,8,128]{1,0,4,3,2:T(2,128)(2,1)} %collective-permute-done.6), kind=kOutput, calls=%fused_computation.15 | convolution fusion | flops 932364288 | bytes 2018304 | tf_op jit(solution)/shard_map/conv_general_dilated | solution.py:51
  340.9 1.6 maximum_bitcast_fusion
  343.7 285.0 %all-reduce.8.cloned.1.call-done = (f32[48,48,3,3,3]{0,1,4,3,2:T(8,128)}, f32[48,48,3,3,3]{0,1,4,3,2:T(8,128)}) async-done(((f32[48,48,3,3,3]{0,1,4,3,2:T(8,128)}, f32[48,48,3,3,3]{0,1,4,3,2:T(8,128)}), (f32[48,48,3,3,3]{0,1,4,3,2:T(8,128)}, f32[48,48,3,3,3]{0,1,4,3,2:T(8,128)})) %all-reduce.8.cloned.1.call-update) | async-done | bytes 497680 | tf_op jit(solution)/shard_map/psum | solution.py:10
  628.7 10.1 %broadcast_select_fusion = f32[8,8,8,17,48]{4,2,3,1,0:T(8,128)S(1)} fusion(pred[8,17]{0,1:T(8,128)(4,1)S(1)} %copy-done.15, bf16[48,48,3,3,3]{1,0,4,3,2:T(8,128)(2,1)S(1)} %copy-done, bf16[48,10,8,1,7,2]{0,4,5,2,1,3:T(8,128)(2,1)S(1)} %slice.57, bf16[48,10,8,1,8,17]{0,4,5,2,1,3:T(8,128)(2,1)S(1)} %copy.98), kind=kOutput, calls=%fused_computation.55 | convolution fusion | flops 996593664 | bytes 2947720 | tf_op jit(solution)/shard_map/conv_general_dilated | solution.py:36
  638.9 0.8 copy.99
  639.7 0.8 copy-done.4
  640.9 2.7 copy.113
  643.5 101.4 %all-reduce.10.cloned.1.call-done = (f32[48,48,3,3,3]{0,1,4,3,2:T(8,128)}, f32[48,48,3,3,3]{0,1,4,3,2:T(8,128)}) async-done(((f32[48,48,3,3,3]{0,1,4,3,2:T(8,128)}, f32[48,48,3,3,3]{0,1,4,3,2:T(8,128)}), (f32[48,48,3,3,3]{0,1,4,3,2:T(8,128)}, f32[48,48,3,3,3]{0,1,4,3,2:T(8,128)})) %all-reduce.10.cloned.1.call-update) | async-done | bytes 497680 | tf_op jit(solution)/shard_map/psum | solution.py:11
  744.9 2.2 copy.114
  747.1 2.2 copy.115
  (69 shorter events, 4.8 us)
Async XLA Ops:
  7.2 48.2 %copy-start = (bf16[48,48,3,3,3]{1,0,4,3,2:T(8,128)(2,1)S(1)}, bf16[48,48,3,3,3]{1,0,4,3,2:T(8,128)(2,1)}, u32[]{:S(2)}) copy-start(bf16[48,48,3,3,3]{1,0,4,3,2:T(8,128)(2,1)} %param.8) | copy-start | bytes 373252
  7.2 21.5 %copy-start.5 = (bf16[1,48,8,8,128]{4,3,2,1,0:T(8,128)(2,1)S(1)}, bf16[1,48,8,8,128]{4,3,2,1,0:T(8,128)(2,1)}, u32[]{:S(2)}) copy-start(bf16[1,48,8,8,128]{4,3,2,1,0:T(8,128)(2,1)} %param.7) | copy-start | bytes 2359300
  7.2 621.5 %all-reduce.8.cloned.1.call-start = ((), (), s32[]{:S(2)}) async-start(), calls=%async_computation | async-start | bytes 2654208 | tf_op jit(solution)/shard_map/psum | solution.py:10
  8.3 22.9 %copy-start.12 = (bf16[1,48,8,8,128]{4,3,2,1,0:T(8,128)(2,1)S(1)}, bf16[1,48,8,8,128]{4,3,2,1,0:T(8,128)(2,1)}, u32[]{:S(2)}) copy-start(bf16[1,48,8,8,128]{4,3,2,1,0:T(8,128)(2,1)} %param.6) | copy-start | bytes 2359300
  8.3 22.9 %collective-permute-start = (bf16[1,48,1,8,128]{4,3,2,1,0:T(8,128)(2,1)S(1)}, bf16[1,48,1,8,128]{4,3,2,1,0:T(8,128)(2,1)S(1)}, u32[]{:S(2)}, u32[]{:S(2)}) collective-permute-start(bf16[1,48,1,8,128]{4,3,2,1,0:T(8,128)(2,1)S(1)} %get-tuple-element.55), channel_id=1, source_target_pairs={{0,32},{32,64},{64,96},{96,128},{128,160},{160,192},{192,224},{1,3... | collective-permute-start | bytes 294920 | tf_op jit(solution)/shard_map/ppermute | solution.py:22
  12.5 18.8 %collective-permute-start.1 = (bf16[1,48,1,8,128]{4,3,2,1,0:T(8,128)(2,1)S(1)}, bf16[1,48,1,8,128]{4,3,2,1,0:T(8,128)(2,1)S(1)}, u32[]{:S(2)}, u32[]{:S(2)}) collective-permute-start(bf16[1,48,1,8,128]{4,3,2,1,0:T(8,128)(2,1)S(1)} %get-tuple-element.56), channel_id=1, source_target_pairs={{32,0},{64,32},{96,64},{128,96},{160,128},{192,160},{224,192},{33,... | collective-permute-start | bytes 294920 | tf_op jit(solution)/shard_map/ppermute | solution.py:24
  15.4 29.1 %collective-permute-start.2 = (bf16[1,48,1,8,128]{4,3,2,1,0:T(8,128)(2,1)}, bf16[1,48,1,8,128]{4,3,2,1,0:T(8,128)(2,1)}, u32[]{:S(2)}, u32[]{:S(2)}) collective-permute-start(bf16[1,48,1,8,128]{4,3,2,1,0:T(8,128)(2,1)} %get-tuple-element.57), channel_id=1, source_target_pairs={{0,32},{32,64},{64,96},{96,128},{128,160},{160,192},{192,224},{1,3... | collective-permute-start | bytes 294920 | tf_op jit(solution)/shard_map/ppermute | solution.py:22
  20.0 24.5 %collective-permute-start.3 = (bf16[1,48,1,8,128]{4,3,2,1,0:T(8,128)(2,1)S(1)}, bf16[1,48,1,8,128]{4,3,2,1,0:T(8,128)(2,1)}, u32[]{:S(2)}, u32[]{:S(2)}) collective-permute-start(bf16[1,48,1,8,128]{4,3,2,1,0:T(8,128)(2,1)S(1)} %get-tuple-element.58), channel_id=1, source_target_pairs={{32,0},{64,32},{96,64},{128,96},{160,128},{192,160},{224,192},{33,... | collective-permute-start | bytes 294920 | tf_op jit(solution)/shard_map/ppermute | solution.py:24
  41.6 2.9 copy-start.6
  42.1 1.5 copy-start.9
  54.0 2.6 copy-start.10
  54.0 2.8 copy-start.13
  54.0 2.8 copy-start.14
  54.5 14.5 %copy-start.8 = (bf16[48,10,8,1,8,17]{0,4,5,2,1,3:T(8,128)(2,1)}, bf16[48,10,8,1,8,17]{0,4,5,2,1,3:T(8,128)(2,1)S(1)}, u32[]{:S(2)}) copy-start(bf16[48,10,8,1,8,17]{0,4,5,2,1,3:T(8,128)(2,1)S(1)} %copy.91) | copy-start | bytes 3133444
  56.8 42.7 %copy-start.16 = (f32[48]{0:T(128)S(1)}, f32[48]{0:T(128)}, u32[]{:S(2)}) copy-start(f32[48]{0:T(128)} %param.10) | copy-start | bytes 580
  56.8 42.8 %copy-start.17 = (f32[48]{0:T(128)S(1)}, f32[48]{0:T(128)}, u32[]{:S(2)}) copy-start(f32[48]{0:T(128)} %param.11) | copy-start | bytes 580
  218.9 7.7 %copy-start.2 = (bf16[48,10,8,1,8,16]{0,2,5,4,1,3:T(8,128)(2,1)S(1)}, bf16[48,10,8,1,8,16]{0,2,5,4,1,3:T(8,128)(2,1)}, u32[]{:S(2)}) copy-start(bf16[48,10,8,1,8,16]{0,2,5,4,1,3:T(8,128)(2,1)} %get-tuple-element.45) | copy-start | bytes 2949124
  220.8 8.2 %copy-start.1 = (bf16[48,10,8,1,8,16]{0,2,5,4,1,3:T(8,128)(2,1)S(1)}, bf16[48,10,8,1,8,16]{0,2,5,4,1,3:T(8,128)(2,1)}, u32[]{:S(2)}) copy-start(bf16[48,10,8,1,8,16]{0,2,5,4,1,3:T(8,128)(2,1)} %get-tuple-element.46) | copy-start | bytes 2949124
  222.0 43.6 %collective-permute-start.6 = (bf16[1,48,1,8,128]{1,0,4,3,2:T(2,128)(2,1)}, bf16[1,48,1,8,128]{1,0,4,3,2:T(2,128)(2,1)}, u32[]{:S(2)}, u32[]{:S(2)}) collective-permute-start(bf16[1,48,1,8,128]{1,0,4,3,2:T(2,128)(2,1)} %bitcast.90), channel_id=1, source_target_pairs={{0,32},{32,64},{64,96},{96,128},{128,160},{160,192},{192,224},{1,3... | collective-permute-start | bytes 294920 | tf_op jit(solution)/shard_map/ppermute | solution.py:22
  225.3 40.3 %collective-permute-start.7 = (bf16[1,48,1,8,128]{1,0,4,3,2:T(2,128)(2,1)}, bf16[1,48,1,8,128]{1,0,4,3,2:T(2,128)(2,1)}, u32[]{:S(2)}, u32[]{:S(2)}) collective-permute-start(bf16[1,48,1,8,128]{1,0,4,3,2:T(2,128)(2,1)} %bitcast.89), channel_id=1, source_target_pairs={{32,0},{64,32},{96,64},{128,96},{160,128},{192,160},{224,192},{33,... | collective-permute-start | bytes 294920 | tf_op jit(solution)/shard_map/ppermute | solution.py:24
  234.0 106.9 %collective-permute-start.4 = (bf16[1,48,1,8,128]{1,3,4,0,2:T(8,128)(2,1)}, bf16[1,48,1,8,128]{1,3,4,0,2:T(8,128)(2,1)}, u32[]{:S(2)}, u32[]{:S(2)}) collective-permute-start(bf16[1,48,1,8,128]{1,3,4,0,2:T(8,128)(2,1)} %slice_bitcast_fusion.3), channel_id=1, source_target_pairs={{0,32},{32,64},{64,96},{96,128},{128,160},{160,192},{192,224},{1,3... | collective-permute-start | bytes 294920 | tf_op jit(solution)/shard_map/ppermute | solution.py:22
  239.5 3.1 copy-start.11
  239.5 101.5 %collective-permute-start.5 = (bf16[1,48,1,8,128]{1,3,4,2,0:T(8,128)(2,1)}, bf16[1,48,1,8,128]{1,3,4,2,0:T(8,128)(2,1)}, u32[]{:S(2)}, u32[]{:S(2)}) collective-permute-start(bf16[1,48,1,8,128]{1,3,4,2,0:T(8,128)(2,1)} %slice_bitcast_fusion.2), channel_id=1, source_target_pairs={{32,0},{64,32},{96,64},{128,96},{160,128},{192,160},{224,192},{33,... | collective-permute-start | bytes 294920 | tf_op jit(solution)/shard_map/ppermute | solution.py:24
  259.3 6.3 copy-start.7
  265.6 75.1 %copy-start.3 = (bf16[8,8,8,17,48]{4,1,3,2,0:T(8,128)(2,1)S(1)}, bf16[8,8,8,17,48]{4,1,3,2,0:T(8,128)(2,1)}, u32[]{:S(2)}) copy-start(bf16[8,8,8,17,48]{4,1,3,2,0:T(8,128)(2,1)} %copy.93) | copy-start | bytes 2506756
  340.7 404.2 %all-reduce.10.cloned.1.call-start = ((), (), s32[]{:S(2)}) async-start(), calls=%async_computation.1 | async-start | bytes 2654208 | tf_op jit(solution)/shard_map/psum | solution.py:11
  343.1 285.6 %copy-start.15 = (pred[8,17]{0,1:T(8,128)(4,1)S(1)}, pred[8,17]{0,1:T(8,128)(4,1)}, u32[]{:S(2)}) copy-start(pred[8,17]{0,1:T(8,128)(4,1)} %constant.35) | copy-start | bytes 412
  638.8 1.6 copy-start.4
Sparse Core Ops, SparseCore 0:
  340.8 287.8 all-reduce.7
  631.7 113.2 all-reduce.9
